TPU v7x, 1024 devices: a whole 8x8x8 slice. The times are simulated.
1024 devices in a mesh: seabed: 64 (over x, z_lo, core), freq: 16 (over y, z_hi).
Axes of the slice: x: 8, y: 8, z: 8 (z_hi: 2, z_lo: 4; z = z_hi * 4 + z_lo), core: 2. Of those that a mesh axis runs over, the one named last changes fastest.
Arguments:
- uplift: bfloat16 [128, 32, 320, 128], P('freq', None, 'seabed'), may hold values from -6 to 6
- coefficient: float32 [320, 128], P('seabed'), may hold values from 0.06 to 0.24
- transfer: float32 [16, 2, 600, 40960], P('freq', None, None, 'seabed'), may hold values from -0.01953125 to 0.01953125
Outputs:
- sensors: float32 [128, 16, 2, 600], P('seabed', 'freq')
All inputs are finite; a program needn't handle non-finite values.
Results may differ from a plain program's by a relative error of at most 0.0003.
Values sent between devices are 32-bit elements; how exact they have to be, the bound alone decides.
A program may use at most 32 MiB of HBM per device.

v0:
```python
import math

import jax
import jax.numpy as jnp
from jax import lax
from jax.sharding import PartitionSpec as P

FD = 1
PASSES = 3


def with_halo(block, sides, width):
    for axis, dim in sides:
        count = lax.axis_size(axis)
        forward = [(i, i + 1) for i in range(count - 1)]
        backward = [(target, source) for source, target in forward]
        low = lax.ppermute(
            lax.slice_in_dim(block, block.shape[dim] - width, None, axis=dim), axis, forward
        )
        high = lax.ppermute(lax.slice_in_dim(block, 0, width, axis=dim), axis, backward)
        block = jnp.concatenate([low, block, high], axis=dim)
    return block


def dft_table(steps_count, freq_count):
    times = jnp.arange(steps_count, dtype=jnp.int32)
    freqs = jnp.arange(freq_count, dtype=jnp.int32)
    phase = (freqs[:, None] * times[None, :] % steps_count).astype(jnp.float32) * (
        2.0 * math.pi / steps_count
    )
    scale = 1.0 / math.sqrt(steps_count)
    return (
        jnp.stack([jnp.cos(phase), -jnp.sin(phase)], 1).reshape(2 * freq_count, steps_count) * scale
    )


def relax(extended, rows_coefficient):
    centre = extended[:, :, 1:-1]
    padded = jnp.pad(centre, ((0, 0), (0, 0), (0, 0), (1, 1)))
    beside = extended[:, :, 2:] + extended[:, :, :-2] + padded[:, :, :, 2:] + padded[:, :, :, :-2]
    return centre + rows_coefficient * (beside - 4.0 * centre)


def shards(uplift, coefficient, transfer):
    field = uplift.astype(jnp.float32)
    vectors, steps_count, rows, width = field.shape
    for step in range(PASSES):
        extended = with_halo(field, (("seabed", 2),), 1)
        field = relax(extended, coefficient)
    flat = field.reshape(vectors, steps_count, rows * width)
    freq_count = FD * lax.axis_size("freq")
    table = dft_table(steps_count, freq_count)
    spectrum = jnp.einsum("ft,vtc->fvc", table, flat, precision=lax.Precision.HIGHEST)
    spectrum = spectrum.reshape(freq_count, 2, vectors, rows * width)
    regrouped = lax.all_to_all(spectrum, "freq", split_axis=0, concat_axis=2, tiled=True)
    products = jnp.einsum("kbvc,kasc->vkbas", regrouped, transfer, precision=lax.Precision.HIGHEST)
    real_part = products[:, :, 0, 0] - products[:, :, 1, 1]
    imag_part = products[:, :, 1, 0] + products[:, :, 0, 1]
    return lax.psum_scatter(
        jnp.stack([real_part, imag_part], 2), "seabed", scatter_dimension=0, tiled=True
    )


def solution(mesh):
    placed = (P("freq", None, "seabed", None), P("seabed", None), P("freq", None, None, "seabed"))
    return jax.shard_map(
        shards,
        mesh=mesh,
        in_specs=placed,
        out_specs=P("seabed", "freq", None, None),
        check_vma=False,
    )
```

profile of v0, /device:TPU:1, one launch (start us, length us, event | category | flops | bytes accessed | tf_op | source)
XLA Modules:
  0.0 616.2 jit_solution(13815086082967932704)
XLA Ops:
  6.5 0.0 copy-start
  6.5 0.0 copy-start.1
  6.5 0.0 all-reduce.6.cloned.1.call-start
  6.5 1.1 fusion.44
  7.6 16.1 %collective-permute-start = (f32[8,32,1,128]{3,1,2,0:T(8,128)S(1)}, f32[8,32,1,128]{3,1,2,0:T(8,128)S(1)}, u32[]{:S(2)}, u32[]{:S(2)}) collective-permute-start(f32[8,32,1,128]{3,1,2,0:T(8,128)S(1)} %get-tuple-element.11), channel_id=1, source_target_pairs={{16,0},{32,16},{48,32},{64,48},{80,64},{96,80},{112,96},{128,112},... | collective-permute-start | bytes 393224 | tf_op jit(solution)/shard_map/ppermute | solution.py:20
  23.7 1.9 collective-permute-start.1
  25.6 1.0 convert_element_type.24
  26.6 0.0 collective-permute-done
  26.7 0.9 collective-permute-done.1
  27.5 0.0 copy-done.1
  27.5 0.4 fusion.9
  28.0 1.9 collective-permute-start.2
  29.9 4.4 collective-permute-start.3
  34.3 0.7 collective-permute-done.2
  35.0 1.2 collective-permute-done.3
  36.2 0.4 fusion.14
  36.6 1.9 collective-permute-start.4
  38.6 4.4 collective-permute-start.5
  42.9 0.1 sine_negate_fusion
  43.0 0.6 collective-permute-done.4
  43.6 2.6 collective-permute-done.5
  46.2 0.4 fusion.19
  46.6 1.4 copy.8
  48.0 2.3 reshape.134
  50.3 1.7 fusion.28
  52.0 0.2 copy.9
  52.2 30.7 %all_to_all.15 = f32[16,2,8,640]{3,2,1,0:T(8,128)S(1)} all-to-all(f32[16,2,8,640]{3,2,1,0:T(8,128)S(1)} %copy.9), channel_id=1, replica_groups=mesh['seabed'=64,'freq'=16] {'freq'}, dimensions={0} | all-to-all | bytes 1310720 | tf_op jit(solution)/shard_map/all_to_all | solution.py:55
  82.9 0.0 copy-done
  82.9 3.1 fusion.2
  86.1 0.1 fusion.26
  86.2 0.9 pad_maximum_fusion.6
  87.0 2.1 copy.11
  89.1 0.0 all-reduce.6.cloned.1.call-update
  89.1 1.3 dynamic-slice
  91.1 516.9 %all-reduce.6.cloned.1.call-done = f32[128,1,2,600]{3,2,1,0:T(2,128)} async-done(((f32[128,1,2,600]{3,2,1,0:T(2,128)}), f32[128,1,2,600]{3,2,1,0:T(2,128)}) %all-reduce.6.cloned.1.call-update) | async-done | bytes 614416
  608.0 1.3 constant_dynamic-slice_fusion
  (2 shorter events, 0.0 us)
Async XLA Ops:
  6.5 76.4 %copy-start = (f32[1,2,600,640]{3,2,1,0:T(8,128)S(1)}, f32[1,2,600,640]{3,2,1,0:T(8,128)}, u32[]{:S(2)}) copy-start(f32[1,2,600,640]{3,2,1,0:T(8,128)} %param.5) | copy-start | bytes 9216004
  6.5 21.0 %copy-start.1 = (f32[5,128]{1,0:T(8,128)S(1)}, f32[5,128]{1,0:T(8,128)}, u32[]{:S(2)}) copy-start(f32[5,128]{1,0:T(8,128)} %param.4) | copy-start | bytes 7684
  6.5 601.5 %all-reduce.6.cloned.1.call-start = ((), (), s32[]{:S(2)}) async-start(), calls=%async_computation.1 | async-start | bytes 1310720
  7.6 19.0 %collective-permute-start = (f32[8,32,1,128]{3,1,2,0:T(8,128)S(1)}, f32[8,32,1,128]{3,1,2,0:T(8,128)S(1)}, u32[]{:S(2)}, u32[]{:S(2)}) collective-permute-start(f32[8,32,1,128]{3,1,2,0:T(8,128)S(1)} %get-tuple-element.11), channel_id=1, source_target_pairs={{16,0},{32,16},{48,32},{64,48},{80,64},{96,80},{112,96},{128,112},... | collective-permute-start | bytes 393224 | tf_op jit(solution)/shard_map/ppermute | solution.py:20
  23.7 3.9 collective-permute-start.1
  28.0 7.0 %collective-permute-start.2 = (f32[8,32,1,128]{3,1,2,0:T(8,128)S(1)}, f32[8,32,1,128]{3,1,2,0:T(8,128)S(1)}, u32[]{:S(2)}, u32[]{:S(2)}) collective-permute-start(f32[8,32,1,128]{3,1,2,0:T(8,128)S(1)} %get-tuple-element.9), channel_id=1, source_target_pairs={{16,0},{32,16},{48,32},{64,48},{80,64},{96,80},{112,96},{128,112},... | collective-permute-start | bytes 393224 | tf_op jit(solution)/shard_map/ppermute | solution.py:20
  29.9 6.3 %collective-permute-start.3 = (f32[8,32,1,128]{3,1,2,0:T(8,128)S(1)}, f32[8,32,1,128]{3,1,2,0:T(8,128)S(1)}, u32[]{:S(2)}, u32[]{:S(2)}) collective-permute-start(f32[8,32,1,128]{3,1,2,0:T(8,128)S(1)} %get-tuple-element.10), channel_id=1, source_target_pairs={{0,16},{16,32},{32,48},{48,64},{64,80},{80,96},{96,112},{112,128},... | collective-permute-start | bytes 393224 | tf_op jit(solution)/shard_map/ppermute | solution.py:17
  36.6 7.0 %collective-permute-start.4 = (f32[8,32,1,128]{3,1,2,0:T(8,128)S(1)}, f32[8,32,1,128]{3,1,2,0:T(8,128)S(1)}, u32[]{:S(2)}, u32[]{:S(2)}) collective-permute-start(f32[8,32,1,128]{3,1,2,0:T(8,128)S(1)} %get-tuple-element.7), channel_id=1, source_target_pairs={{16,0},{32,16},{48,32},{64,48},{80,64},{96,80},{112,96},{128,112},... | collective-permute-start | bytes 393224 | tf_op jit(solution)/shard_map/ppermute | solution.py:20
  38.6 7.7 %collective-permute-start.5 = (f32[8,32,1,128]{3,1,2,0:T(8,128)S(1)}, f32[8,32,1,128]{3,1,2,0:T(8,128)S(1)}, u32[]{:S(2)}, u32[]{:S(2)}) collective-permute-start(f32[8,32,1,128]{3,1,2,0:T(8,128)S(1)} %get-tuple-element.8), channel_id=1, source_target_pairs={{0,16},{16,32},{32,48},{48,64},{64,80},{80,96},{96,112},{112,128},... | collective-permute-start | bytes 393224 | tf_op jit(solution)/shard_map/ppermute | solution.py:17
Sparse Core Ops, SparseCore 0:
  89.2 518.7 all-reduce.5
where the time goes:
time: 617 us; the launch traced here: 616 us
  waiting for transfers between devices  523 us (85%)
  blocking collectives  30.7 us (5%)
  starting transfers between devices  30.5 us (5%)
  between operations  14.2 us (2%)
  local copies, waits for them, and re-layouts  9.59 us (2%)
    unnamed x2, waiting for transfers between devices  517 us
    all_to_all x1, blocking collectives, shards(): lax.all_to_all(spectrum, 'freq', split_axis=0, concat_axis=2, tiled=True)  30.7 us
    ppermute x3, starting transfers between devices, with_halo(): lax.ppermute(lax.slice_in_dim(block, 0, width, axis=dim), axis, backward)  19.9 us
  transfers between devices with their start and end apart: 7, of which 6 were waited for; matrix products, arithmetic and copies ran while one was open for 0% of the time, Pallas kernels for 0%

commit v1 on v0

v1 whole, which is shorter than its diff:
```python
import functools
import math

import jax
import jax.numpy as jnp
import numpy as np
from jax import lax
from jax.experimental import pallas as pl
from jax.experimental.pallas import tpu as pltpu
from jax.sharding import PartitionSpec as P

MESH = pl.DeviceIdType.MESH
PASSES = 3
CORES = 2
Z = 4
GROUPS = 4
F32 = jnp.float32
BF16 = jnp.bfloat16


def split(value):
    high = value.astype(BF16)
    return high, (value - high.astype(F32)).astype(BF16)


def dot_nt(a, b):
    return lax.dot_general(a, b, (((1,), (1,)), ((), ())), preferred_element_type=F32)


def block_table(vectors, steps, freqs):
    phase = (np.arange(freqs)[:, None] * np.arange(steps)[None, :] % steps) * (2.0 * math.pi / steps)
    table = np.stack([np.cos(phase), -np.sin(phase)], 1) / math.sqrt(steps)
    wide = np.einsum("kbt,vw->kbvwt", table, np.eye(vectors))
    wide = wide.reshape(2 * freqs * vectors, vectors * steps).astype(np.float32)
    high = wide.astype(BF16)
    low = (wide - high.astype(np.float32)).astype(BF16)
    return np.stack([high, low])


def kernel(
    dims, x_ref, coef_ref, table_ref, transfer_ref, out_ref,
    ext, coefs, outgoing, incoming, raw, t_high, t_low, l_high, l_low, prod, pair, x_out, x_in, z_out, z_in,
    raw_sem, coef_sems, halo_send, halo_recv, a2a_send, a2a_recv, pair_sems, x_send, x_recv, z_send, z_recv,
):
    X, F, vectors, steps, rows, width, sens, sens_pad = dims
    size = F // GROUPS
    strips = X * Z * CORES
    span = Z * CORES * 2
    s = lax.axis_index("seabed")
    f = lax.axis_index("freq")
    core = s % CORES
    z = (s // CORES) % Z
    x = s // (CORES * Z)
    group_at = x * (CORES * Z)
    local = s % (CORES * Z)
    has_low = s > 0
    has_high = s < strips - 1
    crosses_low = (local == 0) & has_low
    crosses_high = (local == CORES * Z - 1) & has_high

    def x_peer(step):
        return (x + step) % X

    def x_device(at):
        return ((at * Z + z) * CORES + core, f)

    def z_device(at):
        return (group_at + at, f)

    fetch = [pltpu.make_async_copy(transfer_ref.at[0, a], raw.at[a, pl.ds(0, sens)], raw_sem.at[a]) for a in range(2)]
    for copy in fetch:
        copy.start()

    barrier = pltpu.get_barrier_semaphore()

    @pl.loop(1, F)
    def _(step):
        pl.semaphore_signal(barrier, inc=1, device_id=(s, (f + step) % F), device_id_type=MESH)

    @pl.loop(1, X)
    def _(step):
        pl.semaphore_signal(barrier, inc=1, device_id=x_device(x_peer(step)), device_id_type=MESH)

    @pl.loop(1, CORES * Z)
    def _(step):
        pl.semaphore_signal(barrier, inc=1, device_id=z_device((local + step) % (CORES * Z)), device_id_type=MESH)

    @pl.when(crosses_low)
    def _():
        pl.semaphore_signal(barrier, inc=1, device_id=(s - 1, f), device_id_type=MESH)

    @pl.when(crosses_high)
    def _():
        pl.semaphore_signal(barrier, inc=1, device_id=(s + 1, f), device_id_type=MESH)

    for r in range(rows):
        block = x_ref[:, r].reshape(vectors * steps, width)
        ext[PASSES + r] = jnp.dot(table_ref[0], block, preferred_element_type=F32) + jnp.dot(
            table_ref[1], block, preferred_element_type=F32
        )
        coefs[PASSES + r] = jnp.broadcast_to(coef_ref[pl.ds(r, 1), :], (8, width))
    raw[:, pl.ds(sens, sens_pad - sens)] = jnp.zeros((2, sens_pad - sens, raw.shape[2]), F32)

    peers = (F - 1) + (X - 1) + (CORES * Z - 1)
    crosses = crosses_low | crosses_high

    @pl.when(crosses)
    def _():
        pl.semaphore_wait(barrier, peers + 1)

    @pl.when(jnp.logical_not(crosses))
    def _():
        pl.semaphore_wait(barrier, peers)

    lines = 2 * vectors
    LOW, HIGH = 0, 1

    def block_of(g):
        return (f // size + g) % GROUPS

    def coef_copy(side):
        source = coefs.at[pl.ds(rows, PASSES)] if side == LOW else coefs.at[pl.ds(PASSES, PASSES)]
        target = coefs.at[pl.ds(0, PASSES)] if side == LOW else coefs.at[pl.ds(PASSES + rows, PASSES)]
        peer = s + 1 if side == LOW else s - 1
        return pltpu.make_async_remote_copy(
            src_ref=source, dst_ref=target, send_sem=coef_sems.at[side], recv_sem=coef_sems.at[2 + side],
            device_id=(peer, f), device_id_type=MESH,
        )

    def halo_copy(side, g):
        at = pl.ds(pl.multiple_of(block_of(g) * (size * lines), size * lines), size * lines)
        source = ext.at[pl.ds(rows, PASSES), at] if side == LOW else ext.at[pl.ds(PASSES, PASSES), at]
        target = ext.at[pl.ds(0, PASSES), at] if side == LOW else ext.at[pl.ds(PASSES + rows, PASSES), at]
        peer = s + 1 if side == LOW else s - 1
        return pltpu.make_async_remote_copy(
            src_ref=source, dst_ref=target, send_sem=halo_send.at[side, g], recv_sem=halo_recv.at[side, g],
            device_id=(peer, f), device_id_type=MESH,
        )

    @pl.when(has_high)
    def _():
        coef_copy(LOW).start()
        halo_copy(LOW, 0).start()

    @pl.when(has_low)
    def _():
        coef_copy(HIGH).start()
        halo_copy(HIGH, 0).start()

    @pl.loop(1, GROUPS)
    def _(g):
        @pl.when(has_high)
        def _():
            halo_copy(LOW, g).start()

        @pl.when(has_low)
        def _():
            halo_copy(HIGH, g).start()

    @pl.when(jnp.logical_not(has_low))
    def _():
        ext[pl.ds(0, PASSES)] = jnp.zeros((PASSES,) + ext.shape[1:], F32)
        coefs[pl.ds(0, PASSES)] = jnp.zeros((PASSES, 8, width), F32)

    @pl.when(jnp.logical_not(has_high))
    def _():
        ext[pl.ds(PASSES + rows, PASSES)] = jnp.zeros((PASSES,) + ext.shape[1:], F32)
        coefs[pl.ds(PASSES + rows, PASSES)] = jnp.zeros((PASSES, 8, width), F32)

    for copy in fetch:
        copy.wait()
    cells = rows * width
    part = 32

    @pl.loop(0, sens_pad // part)
    def _(i):
        at = pl.ds(pl.multiple_of(i * part, part), part)
        for a in range(2):
            high, low = split(raw[a, at])
            t_high[at, pl.ds(a * cells, cells)] = high
            t_low[at, pl.ds(a * cells, cells)] = low

    @pl.when(has_low)
    def _():
        coef_copy(LOW).wait_recv()

    @pl.when(has_high)
    def _():
        coef_copy(HIGH).wait_recv()

    lane = lax.broadcasted_iota(jnp.int32, (8, width), 1)

    def smoothed(at):
        u = [ext[r, at] for r in range(rows + 2 * PASSES)]
        for p in range(PASSES):
            later = []
            for r in range(1, len(u) - 1):
                left = jnp.where(lane == 0, 0.0, pltpu.roll(u[r], 1, 1))
                right = jnp.where(lane == width - 1, 0.0, pltpu.roll(u[r], width - 1, 1))
                beside = (u[r + 1] + u[r - 1]) + (left + right)
                later.append(u[r] + coefs[r + p] * (beside - 4.0 * u[r]))
            u = later
        return u

    def a2a_copy(k, source):
        return pltpu.make_async_remote_copy(
            src_ref=outgoing.at[k], dst_ref=incoming.at[source], send_sem=a2a_send.at[k], recv_sem=a2a_recv.at[source],
            device_id=(s, k), device_id_type=MESH,
        )

    @pl.loop(0, GROUPS)
    def _(g):
        @pl.when(has_low)
        def _():
            halo_copy(LOW, g).wait_recv()

        @pl.when(has_high)
        def _():
            halo_copy(HIGH, g).wait_recv()

        @pl.loop(0, size)
        def _(j):
            k = block_of(g) * size + (f + j) % size
            for b in range(2):
                at = pl.ds(pl.multiple_of(k * lines + b * vectors, 8), 8)
                for r, value in enumerate(smoothed(at)):
                    outgoing[k, b, r] = value

            @pl.when(k != f)
            def _():
                a2a_copy(k, f).start()

    width_all = rows * width

    @pl.loop(0, F // 2)
    def _(q):
        for own in range(2):
            at = q * 2 + own

            @pl.when(at != f)
            def _():
                pltpu.make_async_remote_copy(
                    src_ref=outgoing.at[at], dst_ref=incoming.at[at], send_sem=a2a_send.at[at],
                    recv_sem=a2a_recv.at[at], device_id=(s, at), device_id_type=MESH,
                ).wait_recv()

            @pl.when(at == f)
            def _():
                incoming[f] = outgoing[f]

        here = pl.ds(pl.multiple_of(q * 16, 16), 16)
        for r in range(rows):
            real = split(incoming[pl.ds(q * 2, 2), 0, r].reshape(16, width))
            imag = split(incoming[pl.ds(q * 2, 2), 1, r].reshape(16, width))
            for store, re, im in ((l_high, real[0], imag[0]), (l_low, real[1], imag[1])):
                store[0, here, pl.ds(r * width, width)] = re
                store[0, here, pl.ds(width_all + r * width, width)] = -im
                store[1, here, pl.ds(r * width, width)] = im
                store[1, here, pl.ds(width_all + r * width, width)] = re

    def products(part_at):
        for first in range(0, sens_pad, 256):
            count = min(256, sens_pad - first)
            at = pl.ds(first, count)
            total = dot_nt(l_high[part_at], t_high[at])
            total += dot_nt(l_low[part_at], t_high[at])
            total += dot_nt(l_high[part_at], t_low[at])
            prod[part_at, :, at] = total

    other = 1 - core
    products(other)
    pair_copy = pltpu.make_async_remote_copy(
        src_ref=prod.at[other], dst_ref=pair, send_sem=pair_sems.at[0], recv_sem=pair_sems.at[1],
        device_id=(group_at + z * CORES + other, f), device_id_type=MESH,
    )
    pair_copy.start()
    products(core)
    pair_copy.wait_recv()

    def x_copy(to, source):
        return pltpu.make_async_remote_copy(
            src_ref=x_out.at[to], dst_ref=x_in.at[source], send_sem=x_send.at[to], recv_sem=x_recv.at[source],
            device_id=x_device(to), device_id_type=MESH,
        )

    @pl.loop(0, X)
    def _(step):
        to = x_peer(step + 1)
        at = pl.ds(pl.multiple_of(to * span, span), span)
        x_out[to] = prod[core, at] + pair[at]

        @pl.when(to != x)
        def _():
            x_copy(to, x).start()

    total = x_out[x]
    for step in range(1, X):
        source = x_peer(step)
        pltpu.make_async_remote_copy(
            src_ref=x_out.at[source], dst_ref=x_in.at[source], send_sem=x_send.at[source], recv_sem=x_recv.at[source],
            device_id=x_device(source), device_id_type=MESH,
        ).wait_recv()
        total += x_in[source]
    for at in range(CORES * Z):
        z_out[at] = total[2 * at : 2 * at + 2]

    def z_copy(to, source):
        return pltpu.make_async_remote_copy(
            src_ref=z_out.at[to], dst_ref=z_in.at[source], send_sem=z_send.at[to], recv_sem=z_recv.at[source],
            device_id=z_device(to), device_id_type=MESH,
        )

    @pl.loop(1, CORES * Z)
    def _(step):
        z_copy((local + step) % (CORES * Z), local).start()

    z_in[local] = z_out[local]

    @pl.loop(1, CORES * Z)
    def _(step):
        source = (local + step) % (CORES * Z)
        z_copy(source, source).wait_recv()

    for part_at in range(2):
        result = z_in[part_at]
        for at in range(1, Z):
            result += z_in[at * CORES + part_at]
        for v in range(2):
            out_ref[v, 0, pl.ds(part_at, 1)] = result[v : v + 1, :sens]

    @pl.when(has_high)
    def _():
        coef_copy(LOW).wait_send()

    @pl.when(has_low)
    def _():
        coef_copy(HIGH).wait_send()

    @pl.loop(0, GROUPS)
    def _(g):
        @pl.when(has_high)
        def _():
            halo_copy(LOW, g).wait_send()

        @pl.when(has_low)
        def _():
            halo_copy(HIGH, g).wait_send()

    @pl.loop(1, F)
    def _(step):
        a2a_copy((f + step) % F, f).wait_send()

    pair_copy.wait_send()

    @pl.loop(1, X)
    def _(step):
        x_copy(x_peer(step), x).wait_send()

    @pl.loop(1, CORES * Z)
    def _(step):
        z_copy((local + step) % (CORES * Z), local).wait_send()


def shards(uplift, coefficient, transfer):
    vectors, steps, rows, width = uplift.shape
    sens = transfer.shape[2]
    F = lax.axis_size("freq")
    strips = lax.axis_size("seabed")
    X = strips // (Z * CORES)
    all_vectors = vectors * F
    span = Z * CORES * 2
    sens_pad = -(-sens // 128) * 128
    cells = rows * width
    dims = (X, F, vectors, steps, rows, width, sens, sens_pad)
    table = jnp.asarray(block_table(vectors, steps, F))
    field = jnp.transpose(uplift, (0, 2, 1, 3))
    dma = pltpu.SemaphoreType.DMA
    vmem = pl.BlockSpec(memory_space=pltpu.VMEM)
    return pl.pallas_call(
        functools.partial(kernel, dims),
        out_shape=jax.ShapeDtypeStruct((2, 1, 2, sens), F32),
        in_specs=[vmem, vmem, vmem, pl.BlockSpec(memory_space=pl.ANY)],
        out_specs=vmem,
        scratch_shapes=[
            pltpu.VMEM((rows + 2 * PASSES, 2 * F * vectors, width), F32),
            pltpu.VMEM((rows + 2 * PASSES, 8, width), F32),
            pltpu.VMEM((F, 2, rows, vectors, width), F32),
            pltpu.VMEM((F, 2, rows, vectors, width), F32),
            pltpu.VMEM((2, sens_pad, cells), F32),
            pltpu.VMEM((sens_pad, 2 * cells), BF16),
            pltpu.VMEM((sens_pad, 2 * cells), BF16),
            pltpu.VMEM((2, all_vectors, 2 * cells), BF16),
            pltpu.VMEM((2, all_vectors, 2 * cells), BF16),
            pltpu.VMEM((2, all_vectors, sens_pad), F32),
            pltpu.VMEM((all_vectors, sens_pad), F32),
            pltpu.VMEM((X, span, sens_pad), F32),
            pltpu.VMEM((X, span, sens_pad), F32),
            pltpu.VMEM((CORES * Z, 2, sens_pad), F32),
            pltpu.VMEM((CORES * Z, 2, sens_pad), F32),
            dma((2,)),
            dma((4,)),
            dma((2, GROUPS)),
            dma((2, GROUPS)),
            dma((F,)),
            dma((F,)),
            dma((2,)),
            dma((X,)),
            dma((X,)),
            dma((CORES * Z,)),
            dma((CORES * Z,)),
        ],
        compiler_params=pltpu.CompilerParams(
            collective_id=0, has_side_effects=True, vmem_limit_bytes=40 * 1024 * 1024
        ),
    )(field, coefficient, table, transfer)


def solution(mesh):
    placed = (P("freq", None, "seabed", None), P("seabed", None), P("freq", None, None, "seabed"))
    return jax.shard_map(
        shards,
        mesh=mesh,
        in_specs=placed,
        out_specs=P("seabed", "freq", None, None),
        check_vma=False,
    )
```

time: 617 us -> 79.3 us (0.13)
  waiting for transfers between devices: 523 us -> 0 us
  Pallas kernels: 0 us -> 72.8 us
  blocking collectives: 30.7 us -> 0 us
  starting transfers between devices: 30.5 us -> 0 us
  between operations: 14.2 us -> 0.01 us
    unnamed x2 -> x0, waiting for transfers between devices: 517 us -> none
    pallas_call x0 -> x1, Pallas kernels: none -> 72.8 us  [shards(): pl.pallas_call(functools.partial(kernel, dims), out_shape=jax.ShapeDtypeS...]
    all_to_all x1 -> x0, blocking collectives: 30.7 us -> none  [shards(): lax.all_to_all(spectrum, 'freq', split_axis=0, concat_axis=2, tiled=True)]
    ppermute x6 -> x0, starting transfers between devices: 30.5 us -> none  [the longest x3 19.9 us: with_halo(): lax.ppermute(lax.slice_in_dim(block, 0, width, axis=dim), axis, backward)]
  transfers between devices with their start and end apart: 7 -> 0, of which waited for: 6 -> 0; matrix products, arithmetic and copies ran while one was open for 0% -> 0% of each run, Pallas kernels for 0% -> 0%
where the time goes in v1:
time: 79.3 us; the launch traced here: 77.9 us
  Pallas kernels  72.8 us (92%)
  local copies, waits for them, and re-layouts  5.08 us (6%)
    pallas_call x1, Pallas kernels, shards(): pl.pallas_call(functools.partial(kernel, dims), out_shape=jax.ShapeDtypeS...  72.8 us
    unnamed x9, local copies, waits for them, and re-layouts  5.08 us

profile of v1, /device:TPU:1, one launch (start us, length us, event | category | flops | bytes accessed | tf_op | source)
XLA Modules:
  0.0 77.9 jit_solution(1226067990688654872)
XLA Ops:
  0.0 0.0 copy-start
  0.0 1.9 %copy-done = f32[1,2,600,640]{3,2,1,0:T(8,128)S(1)} copy-done((f32[1,2,600,640]{3,2,1,0:T(8,128)S(1)}, f32[1,2,600,640]{3,2,1,0:T(8,128)}, u32[]{:S(2)}) %copy-start) | copy-done | bytes 3072024
  1.9 0.0 copy-start.1
  1.9 1.0 %copy-done.1 = bf16[8,32,5,128]{3,1,2,0:T(8,128)(2,1)S(1)} copy-done((bf16[8,32,5,128]{3,1,2,0:T(8,128)(2,1)S(1)}, bf16[8,32,5,128]{3,1,2,0:T(8,128)(2,1)}, u32[]{:S(2)}) %copy-start.1) | copy-done | bytes 327704
  2.8 0.0 copy-start.2
  2.8 0.9 %copy-done.2 = bf16[2,256,256]{2,1,0:T(8,128)(2,1)S(1)} copy-done((bf16[2,256,256]{2,1,0:T(8,128)(2,1)S(1)}, bf16[2,256,256]{2,1,0:T(8,128)(2,1)}, u32[]{:S(2)}) %copy-start.2) | copy-done | bytes 262168
  3.8 0.0 copy-start.3
  3.8 0.7 copy-done.3
  4.5 72.8 %shard_map.46 = f32[2,1,2,600]{3,2,1,0:T(2,128)S(1)} custom-call(bf16[8,5,32,128]{3,2,1,0:T(8,128)(2,1)S(1)} %bitcast.1, f32[5,128]{1,0:T(8,128)S(1)} %copy-done.3, bf16[2,256,256]{2,1,0:T(8,128)(2,1)S(1)} %copy-done.2, f32[1,2,600,640]{3,2,1,0:T(8,128)S(1)} %copy-done), custom_call_target="tpu_custom_call" | custom-call | tf_op jit(solution)/shard_map/pallas_call | solution.py:379
  77.3 0.6 copy.6
Async XLA Ops:
  0.0 1.9 %copy-start = (f32[1,2,600,640]{3,2,1,0:T(8,128)S(1)}, f32[1,2,600,640]{3,2,1,0:T(8,128)}, u32[]{:S(2)}) copy-start(f32[1,2,600,640]{3,2,1,0:T(8,128)} %transfer_ref.1) | copy-start | bytes 9216004
  1.9 1.0 %copy-start.1 = (bf16[8,32,5,128]{3,1,2,0:T(8,128)(2,1)S(1)}, bf16[8,32,5,128]{3,1,2,0:T(8,128)(2,1)}, u32[]{:S(2)}) copy-start(bf16[8,32,5,128]{3,1,2,0:T(8,128)(2,1)} %param.4) | copy-start | bytes 983044
  2.8 0.9 %copy-start.2 = (bf16[2,256,256]{2,1,0:T(8,128)(2,1)S(1)}, bf16[2,256,256]{2,1,0:T(8,128)(2,1)}, u32[]{:S(2)}) copy-start(bf16[2,256,256]{2,1,0:T(8,128)(2,1)} %constant.2.clone.table_ref) | copy-start | bytes 786436
  3.8 0.7 copy-start.3

commit v2 on v1

--- a/solution.py
+++ b/solution.py
@@ -14,6 +14,7 @@
 CORES = 2
 Z = 4
 GROUPS = 4
+AHEAD = 2
 F32 = jnp.float32
 BF16 = jnp.bfloat16
 
@@ -38,12 +39,13 @@
 
 
 def kernel(
-    dims, x_ref, coef_ref, table_ref, transfer_ref, out_ref,
-    ext, coefs, outgoing, incoming, raw, t_high, t_low, l_high, l_low, prod, pair, x_out, x_in, z_out, z_in,
-    raw_sem, coef_sems, halo_send, halo_recv, a2a_send, a2a_recv, pair_sems, x_send, x_recv, z_send, z_recv,
+    dims, x_hbm, coef_hbm, table_hbm, transfer_ref, out_ref,
+    x_ref, coef_ref, table_ref, ext, coefs, outgoing, incoming, raw, t_high, t_low, parts, prod, pair, x_out, x_in, z_out, z_in,
+    in_sems, raw_sem, coef_sems, halo_send, halo_recv, a2a_send, a2a_recv, pair_send, pair_recv, x_send, x_recv, z_send, z_recv,
 ):
     X, F, vectors, steps, rows, width, sens, sens_pad = dims
     size = F // GROUPS
+    block_rows = size * vectors
     strips = X * Z * CORES
     span = Z * CORES * 2
     s = lax.axis_index("seabed")
@@ -67,31 +69,40 @@
     def z_device(at):
         return (group_at + at, f)
 
+    first = [
+        pltpu.make_async_copy(source, target, in_sems.at[i])
+        for i, (source, target) in enumerate(((x_hbm, x_ref), (table_hbm, table_ref), (coef_hbm, coef_ref)))
+    ]
+    for copy in first:
+        copy.start()
     fetch = [pltpu.make_async_copy(transfer_ref.at[0, a], raw.at[a, pl.ds(0, sens)], raw_sem.at[a]) for a in range(2)]
+
+    barrier = pltpu.get_barrier_semaphore()
+
+    @pl.when(crosses_low)
+    def _():
+        pl.semaphore_signal(barrier, inc=1, device_id=(s - 1, f), device_id_type=MESH)
+
+    @pl.when(crosses_high)
+    def _():
+        pl.semaphore_signal(barrier, inc=1, device_id=(s + 1, f), device_id_type=MESH)
+
+    @pl.loop(1, F)
+    def _(step):
+        pl.semaphore_signal(barrier, inc=1, device_id=(s, (f + step) % F), device_id_type=MESH)
+
+    @pl.loop(1, X)
+    def _(step):
+        pl.semaphore_signal(barrier, inc=1, device_id=x_device(x_peer(step)), device_id_type=MESH)
+
+    @pl.loop(1, CORES * Z)
+    def _(step):
+        pl.semaphore_signal(barrier, inc=1, device_id=z_device((local + step) % (CORES * Z)), device_id_type=MESH)
+
     for copy in fetch:
         copy.start()
-
-    barrier = pltpu.get_barrier_semaphore()
-
-    @pl.loop(1, F)
-    def _(step):
-        pl.semaphore_signal(barrier, inc=1, device_id=(s, (f + step) % F), device_id_type=MESH)
-
-    @pl.loop(1, X)
-    def _(step):
-        pl.semaphore_signal(barrier, inc=1, device_id=x_device(x_peer(step)), device_id_type=MESH)
-
-    @pl.loop(1, CORES * Z)
-    def _(step):
-        pl.semaphore_signal(barrier, inc=1, device_id=z_device((local + step) % (CORES * Z)), device_id_type=MESH)
-
-    @pl.when(crosses_low)
-    def _():
-        pl.semaphore_signal(barrier, inc=1, device_id=(s - 1, f), device_id_type=MESH)
-
-    @pl.when(crosses_high)
-    def _():
-        pl.semaphore_signal(barrier, inc=1, device_id=(s + 1, f), device_id_type=MESH)
+    for copy in first:
+        copy.wait()
 
     for r in range(rows):
         block = x_ref[:, r].reshape(vectors * steps, width)
@@ -115,8 +126,8 @@
     lines = 2 * vectors
     LOW, HIGH = 0, 1
 
-    def block_of(g):
-        return (f // size + g) % GROUPS
+    def block_of(g, x_at):
+        return (f // size + g + x_at * GROUPS // X) % GROUPS
 
     def coef_copy(side):
         source = coefs.at[pl.ds(rows, PASSES)] if side == LOW else coefs.at[pl.ds(PASSES, PASSES)]
@@ -127,8 +138,8 @@
             device_id=(peer, f), device_id_type=MESH,
         )
 
-    def halo_copy(side, g):
-        at = pl.ds(pl.multiple_of(block_of(g) * (size * lines), size * lines), size * lines)
+    def halo_copy(side, g, x_at):
+        at = pl.ds(pl.multiple_of(block_of(g, x_at) * (size * lines), size * lines), size * lines)
         source = ext.at[pl.ds(rows, PASSES), at] if side == LOW else ext.at[pl.ds(PASSES, PASSES), at]
         target = ext.at[pl.ds(0, PASSES), at] if side == LOW else ext.at[pl.ds(PASSES + rows, PASSES), at]
         peer = s + 1 if side == LOW else s - 1
@@ -137,25 +148,25 @@
             device_id=(peer, f), device_id_type=MESH,
         )
 
+    def halo_start(g):
+        @pl.when(has_high)
+        def _():
+            halo_copy(LOW, g, (s + 1) // (CORES * Z)).start()
+
+        @pl.when(has_low)
+        def _():
+            halo_copy(HIGH, g, (s - 1) // (CORES * Z)).start()
+
     @pl.when(has_high)
     def _():
         coef_copy(LOW).start()
-        halo_copy(LOW, 0).start()
 
     @pl.when(has_low)
     def _():
         coef_copy(HIGH).start()
-        halo_copy(HIGH, 0).start()
-
-    @pl.loop(1, GROUPS)
-    def _(g):
-        @pl.when(has_high)
-        def _():
-            halo_copy(LOW, g).start()
-
-        @pl.when(has_low)
-        def _():
-            halo_copy(HIGH, g).start()
+
+    for g in range(min(AHEAD, GROUPS)):
+        halo_start(g)
 
     @pl.when(jnp.logical_not(has_low))
     def _():
@@ -212,15 +223,19 @@
     def _(g):
         @pl.when(has_low)
         def _():
-            halo_copy(LOW, g).wait_recv()
+            halo_copy(LOW, g, x).wait_recv()
 
         @pl.when(has_high)
         def _():
-            halo_copy(HIGH, g).wait_recv()
+            halo_copy(HIGH, g, x).wait_recv()
+
+        @pl.when(g + AHEAD < GROUPS)
+        def _():
+            halo_start(g + AHEAD)
 
         @pl.loop(0, size)
         def _(j):
-            k = block_of(g) * size + (f + j) % size
+            k = block_of(g, x) * size + (f + j) % size
             for b in range(2):
                 at = pl.ds(pl.multiple_of(k * lines + b * vectors, 8), 8)
                 for r, value in enumerate(smoothed(at)):
@@ -230,12 +245,27 @@
             def _():
                 a2a_copy(k, f).start()
 
-    width_all = rows * width
-
-    @pl.loop(0, F // 2)
-    def _(q):
-        for own in range(2):
-            at = q * 2 + own
+            @pl.when(k == f)
+            def _():
+                incoming[f] = outgoing[f]
+
+    other = 1 - core
+
+    def arrived(g):
+        return (f // size + 2 * GROUPS - g - x * GROUPS // X) % GROUPS
+
+    def rows_of(block):
+        return pl.ds(pl.multiple_of(block * block_rows, block_rows), block_rows)
+
+    def pair_copy(block):
+        return pltpu.make_async_remote_copy(
+            src_ref=prod.at[other, rows_of(block)], dst_ref=pair.at[rows_of(block)], send_sem=pair_send.at[block],
+            recv_sem=pair_recv.at[block], device_id=(group_at + z * CORES + other, f), device_id_type=MESH,
+        )
+
+    def products(block):
+        for j in range(size):
+            at = block * size + j
 
             @pl.when(at != f)
             def _():
@@ -244,38 +274,25 @@
                     recv_sem=a2a_recv.at[at], device_id=(s, at), device_id_type=MESH,
                 ).wait_recv()
 
-            @pl.when(at == f)
-            def _():
-                incoming[f] = outgoing[f]
-
-        here = pl.ds(pl.multiple_of(q * 16, 16), 16)
-        for r in range(rows):
-            real = split(incoming[pl.ds(q * 2, 2), 0, r].reshape(16, width))
-            imag = split(incoming[pl.ds(q * 2, 2), 1, r].reshape(16, width))
-            for store, re, im in ((l_high, real[0], imag[0]), (l_low, real[1], imag[1])):
-                store[0, here, pl.ds(r * width, width)] = re
-                store[0, here, pl.ds(width_all + r * width, width)] = -im
-                store[1, here, pl.ds(r * width, width)] = im
-                store[1, here, pl.ds(width_all + r * width, width)] = re
-
-    def products(part_at):
+        for q in range(size // 2):
+            here = pl.ds(q * 16, 16)
+            for r in range(rows):
+                real = split(incoming[pl.ds(block * size + q * 2, 2), 0, r].reshape(16, width))
+                imag = split(incoming[pl.ds(block * size + q * 2, 2), 1, r].reshape(16, width))
+                for i in range(2):
+                    parts[i, 0, here, pl.ds(r * width, width)] = real[i]
+                    parts[i, 0, here, pl.ds(cells + r * width, width)] = -imag[i]
+                    parts[i, 1, here, pl.ds(r * width, width)] = imag[i]
+                    parts[i, 1, here, pl.ds(cells + r * width, width)] = real[i]
+        both = parts[...].reshape(4 * block_rows, 2 * cells)
         for first in range(0, sens_pad, 256):
-            count = min(256, sens_pad - first)
-            at = pl.ds(first, count)
-            total = dot_nt(l_high[part_at], t_high[at])
-            total += dot_nt(l_low[part_at], t_high[at])
-            total += dot_nt(l_high[part_at], t_low[at])
-            prod[part_at, :, at] = total
-
-    other = 1 - core
-    products(other)
-    pair_copy = pltpu.make_async_remote_copy(
-        src_ref=prod.at[other], dst_ref=pair, send_sem=pair_sems.at[0], recv_sem=pair_sems.at[1],
-        device_id=(group_at + z * CORES + other, f), device_id_type=MESH,
-    )
-    pair_copy.start()
-    products(core)
-    pair_copy.wait_recv()
+            at = pl.ds(first, min(256, sens_pad - first))
+            all_high = dot_nt(both, t_high[at])
+            total = all_high[: 2 * block_rows] + all_high[2 * block_rows :]
+            total += dot_nt(both[: 2 * block_rows], t_low[at])
+            prod[0, rows_of(block), at] = total[:block_rows]
+            prod[1, rows_of(block), at] = total[block_rows:]
+        pair_copy(block).start()
 
     def x_copy(to, source):
         return pltpu.make_async_remote_copy(
@@ -283,15 +300,26 @@
             device_id=x_device(to), device_id_type=MESH,
         )
 
-    @pl.loop(0, X)
-    def _(step):
-        to = x_peer(step + 1)
-        at = pl.ds(pl.multiple_of(to * span, span), span)
-        x_out[to] = prod[core, at] + pair[at]
-
-        @pl.when(to != x)
-        def _():
-            x_copy(to, x).start()
+    def pass_on(block):
+        pair_copy(block).wait_recv()
+        for i in range(block_rows // span):
+            to = block * (block_rows // span) + i
+            at = pl.ds(pl.multiple_of(to * span, span), span)
+            x_out[to] = prod[core, at] + pair[at]
+
+            @pl.when(to != x)
+            def _():
+                x_copy(to, x).start()
+
+    @pl.loop(0, GROUPS)
+    def _(g):
+        products(arrived(g))
+
+        @pl.when(g > 0)
+        def _():
+            pass_on(arrived(g - 1))
+
+    pass_on(arrived(GROUPS - 1))
 
     total = x_out[x]
     for step in range(1, X):
@@ -340,17 +368,19 @@
     def _(g):
         @pl.when(has_high)
         def _():
-            halo_copy(LOW, g).wait_send()
+            halo_copy(LOW, g, (s + 1) // (CORES * Z)).wait_send()
 
         @pl.when(has_low)
         def _():
-            halo_copy(HIGH, g).wait_send()
+            halo_copy(HIGH, g, (s - 1) // (CORES * Z)).wait_send()
 
     @pl.loop(1, F)
     def _(step):
         a2a_copy((f + step) % F, f).wait_send()
 
-    pair_copy.wait_send()
+    @pl.loop(0, GROUPS)
+    def _(block):
+        pair_copy(block).wait_send()
 
     @pl.loop(1, X)
     def _(step):
@@ -379,9 +409,12 @@
     return pl.pallas_call(
         functools.partial(kernel, dims),
         out_shape=jax.ShapeDtypeStruct((2, 1, 2, sens), F32),
-        in_specs=[vmem, vmem, vmem, pl.BlockSpec(memory_space=pl.ANY)],
+        in_specs=[pl.BlockSpec(memory_space=pltpu.HBM)] * 4,
         out_specs=vmem,
         scratch_shapes=[
+            pltpu.VMEM((vectors, rows, steps, width), BF16),
+            pltpu.VMEM((rows, width), F32),
+            pltpu.VMEM(table.shape, BF16),
             pltpu.VMEM((rows + 2 * PASSES, 2 * F * vectors, width), F32),
             pltpu.VMEM((rows + 2 * PASSES, 8, width), F32),
             pltpu.VMEM((F, 2, rows, vectors, width), F32),
@@ -389,28 +422,29 @@
             pltpu.VMEM((2, sens_pad, cells), F32),
             pltpu.VMEM((sens_pad, 2 * cells), BF16),
             pltpu.VMEM((sens_pad, 2 * cells), BF16),
-            pltpu.VMEM((2, all_vectors, 2 * cells), BF16),
-            pltpu.VMEM((2, all_vectors, 2 * cells), BF16),
+            pltpu.VMEM((2, 2, all_vectors // GROUPS, 2 * cells), BF16),
             pltpu.VMEM((2, all_vectors, sens_pad), F32),
             pltpu.VMEM((all_vectors, sens_pad), F32),
             pltpu.VMEM((X, span, sens_pad), F32),
             pltpu.VMEM((X, span, sens_pad), F32),
             pltpu.VMEM((CORES * Z, 2, sens_pad), F32),
             pltpu.VMEM((CORES * Z, 2, sens_pad), F32),
+            dma((3,)),
             dma((2,)),
             dma((4,)),
             dma((2, GROUPS)),
             dma((2, GROUPS)),
             dma((F,)),
             dma((F,)),
-            dma((2,)),
+            dma((GROUPS,)),
+            dma((GROUPS,)),
             dma((X,)),
             dma((X,)),
             dma((CORES * Z,)),
             dma((CORES * Z,)),
         ],
         compiler_params=pltpu.CompilerParams(
-            collective_id=0, has_side_effects=True, vmem_limit_bytes=40 * 1024 * 1024
+            collective_id=0, has_side_effects=True, vmem_limit_bytes=61 * 1024 * 1024
         ),
     )(field, coefficient, table, transfer)
 

time: 79.3 us -> 71.9 us (0.907); the launches traced: 77.9 us -> 71.4 us
  local copies, waits for them, and re-layouts: 5.08 us -> 1.3 us
  Pallas kernels: 72.8 us -> 70.1 us
    unnamed x9 -> x1, local copies, waits for them, and re-layouts: 5.08 us -> 1.3 us
    pallas_call x1, Pallas kernels: 72.8 us -> 70.1 us  [shards(): pl.pallas_call(functools.partial(kernel, dims), out_shape=jax.ShapeDtypeS...]
where the time goes in v2:
time: 71.9 us; the launch traced here: 71.4 us
  Pallas kernels  70.1 us (97%)
  local copies, waits for them, and re-layouts  1.3 us (2%)
    pallas_call x1, Pallas kernels, shards(): pl.pallas_call(functools.partial(kernel, dims), out_shape=jax.ShapeDtypeS...  70.1 us

profile of v2, /device:TPU:1, one launch (start us, length us, event | category | flops | bytes accessed | tf_op | source)
XLA Modules:
  0.0 71.4 jit_solution(15620036520842888931)
XLA Ops:
  0.0 70.1 %shard_map.46 = f32[2,1,2,600]{3,2,1,0:T(2,128)} custom-call(bf16[8,5,32,128]{3,2,1,0:T(8,128)(2,1)} %bitcast.1, f32[5,128]{1,0:T(8,128)} %coef_hbm.1, bf16[2,256,256]{2,1,0:T(8,128)(2,1)} %constant.2.clone.table_hbm, f32[1,2,600,640]{3,2,1,0:T(8,128)} %transfer_ref.1), custom_call_target="tpu_custom_call" | custom-call | tf_op jit(solution)/shard_map/pallas_call | solution.py:409
  70.1 1.3 %copy.6 = f32[2,1,2,600]{3,2,1,0:T(2,128)} copy(f32[2,1,2,600]{3,2,1,0:T(2,128)} %shard_map.46) | data formatting | bytes 19200

commit v3 on v2

--- a/solution.py
+++ b/solution.py
@@ -14,7 +14,7 @@
 CORES = 2
 Z = 4
 GROUPS = 4
-AHEAD = 2
+AHEAD = 16
 F32 = jnp.float32
 BF16 = jnp.bfloat16
 
@@ -47,7 +47,6 @@
     size = F // GROUPS
     block_rows = size * vectors
     strips = X * Z * CORES
-    span = Z * CORES * 2
     s = lax.axis_index("seabed")
     f = lax.axis_index("freq")
     core = s % CORES
@@ -126,8 +125,12 @@
     lines = 2 * vectors
     LOW, HIGH = 0, 1
 
-    def block_of(g, x_at):
-        return (f // size + g + x_at * GROUPS // X) % GROUPS
+    def target_of(step):
+        g, i = step // size, step % size
+        return (f // GROUPS + i) % size * GROUPS + (f % GROUPS + g + i) % GROUPS
+
+    def source_of(g, i):
+        return (f // GROUPS + size - i) % size * GROUPS + (f % GROUPS + 2 * F - g - i) % GROUPS
 
     def coef_copy(side):
         source = coefs.at[pl.ds(rows, PASSES)] if side == LOW else coefs.at[pl.ds(PASSES, PASSES)]
@@ -138,24 +141,24 @@
             device_id=(peer, f), device_id_type=MESH,
         )
 
-    def halo_copy(side, g, x_at):
-        at = pl.ds(pl.multiple_of(block_of(g, x_at) * (size * lines), size * lines), size * lines)
+    def halo_copy(side, step):
+        at = pl.ds(pl.multiple_of(target_of(step) * lines, lines), lines)
         source = ext.at[pl.ds(rows, PASSES), at] if side == LOW else ext.at[pl.ds(PASSES, PASSES), at]
         target = ext.at[pl.ds(0, PASSES), at] if side == LOW else ext.at[pl.ds(PASSES + rows, PASSES), at]
         peer = s + 1 if side == LOW else s - 1
         return pltpu.make_async_remote_copy(
-            src_ref=source, dst_ref=target, send_sem=halo_send.at[side, g], recv_sem=halo_recv.at[side, g],
+            src_ref=source, dst_ref=target, send_sem=halo_send.at[side, step], recv_sem=halo_recv.at[side, step],
             device_id=(peer, f), device_id_type=MESH,
         )
 
-    def halo_start(g):
+    def halo_start(step):
         @pl.when(has_high)
         def _():
-            halo_copy(LOW, g, (s + 1) // (CORES * Z)).start()
+            halo_copy(LOW, step).start()
 
         @pl.when(has_low)
         def _():
-            halo_copy(HIGH, g, (s - 1) // (CORES * Z)).start()
+            halo_copy(HIGH, step).start()
 
     @pl.when(has_high)
     def _():
@@ -165,8 +168,9 @@
     def _():
         coef_copy(HIGH).start()
 
-    for g in range(min(AHEAD, GROUPS)):
-        halo_start(g)
+    @pl.loop(0, min(AHEAD, F))
+    def _(step):
+        halo_start(step)
 
     @pl.when(jnp.logical_not(has_low))
     def _():
@@ -219,53 +223,45 @@
             device_id=(s, k), device_id_type=MESH,
         )
 
-    @pl.loop(0, GROUPS)
-    def _(g):
+    @pl.loop(0, F)
+    def _(step):
         @pl.when(has_low)
         def _():
-            halo_copy(LOW, g, x).wait_recv()
+            halo_copy(LOW, step).wait_recv()
 
         @pl.when(has_high)
         def _():
-            halo_copy(HIGH, g, x).wait_recv()
-
-        @pl.when(g + AHEAD < GROUPS)
-        def _():
-            halo_start(g + AHEAD)
-
-        @pl.loop(0, size)
-        def _(j):
-            k = block_of(g, x) * size + (f + j) % size
-            for b in range(2):
-                at = pl.ds(pl.multiple_of(k * lines + b * vectors, 8), 8)
-                for r, value in enumerate(smoothed(at)):
-                    outgoing[k, b, r] = value
-
-            @pl.when(k != f)
-            def _():
-                a2a_copy(k, f).start()
-
-            @pl.when(k == f)
-            def _():
-                incoming[f] = outgoing[f]
+            halo_copy(HIGH, step).wait_recv()
+
+        @pl.when(step + AHEAD < F)
+        def _():
+            halo_start(step + AHEAD)
+
+        k = target_of(step)
+        for b in range(2):
+            at = pl.ds(pl.multiple_of(k * lines + b * vectors, 8), 8)
+            for r, value in enumerate(smoothed(at)):
+                outgoing[k, b, r] = value
+
+        @pl.when(k != f)
+        def _():
+            a2a_copy(k, f).start()
+
+        @pl.when(k == f)
+        def _():
+            incoming[f] = outgoing[f]
 
     other = 1 - core
 
-    def arrived(g):
-        return (f // size + 2 * GROUPS - g - x * GROUPS // X) % GROUPS
-
-    def rows_of(block):
-        return pl.ds(pl.multiple_of(block * block_rows, block_rows), block_rows)
-
-    def pair_copy(block):
-        return pltpu.make_async_remote_copy(
-            src_ref=prod.at[other, rows_of(block)], dst_ref=pair.at[rows_of(block)], send_sem=pair_send.at[block],
-            recv_sem=pair_recv.at[block], device_id=(group_at + z * CORES + other, f), device_id_type=MESH,
-        )
-
-    def products(block):
-        for j in range(size):
-            at = block * size + j
+    def pair_copy(g):
+        return pltpu.make_async_remote_copy(
+            src_ref=prod.at[g, other], dst_ref=pair.at[g], send_sem=pair_send.at[g], recv_sem=pair_recv.at[g],
+            device_id=(group_at + z * CORES + other, f), device_id_type=MESH,
+        )
+
+    def products(g):
+        for i in range(size):
+            at = source_of(g, i)
 
             @pl.when(at != f)
             def _():
@@ -276,9 +272,10 @@
 
         for q in range(size // 2):
             here = pl.ds(q * 16, 16)
+            one, two = source_of(g, 2 * q), source_of(g, 2 * q + 1)
             for r in range(rows):
-                real = split(incoming[pl.ds(block * size + q * 2, 2), 0, r].reshape(16, width))
-                imag = split(incoming[pl.ds(block * size + q * 2, 2), 1, r].reshape(16, width))
+                real = split(jnp.concatenate([incoming[one, 0, r], incoming[two, 0, r]], axis=0))
+                imag = split(jnp.concatenate([incoming[one, 1, r], incoming[two, 1, r]], axis=0))
                 for i in range(2):
                     parts[i, 0, here, pl.ds(r * width, width)] = real[i]
                     parts[i, 0, here, pl.ds(cells + r * width, width)] = -imag[i]
@@ -290,47 +287,75 @@
             all_high = dot_nt(both, t_high[at])
             total = all_high[: 2 * block_rows] + all_high[2 * block_rows :]
             total += dot_nt(both[: 2 * block_rows], t_low[at])
-            prod[0, rows_of(block), at] = total[:block_rows]
-            prod[1, rows_of(block), at] = total[block_rows:]
-        pair_copy(block).start()
-
-    def x_copy(to, source):
-        return pltpu.make_async_remote_copy(
-            src_ref=x_out.at[to], dst_ref=x_in.at[source], send_sem=x_send.at[to], recv_sem=x_recv.at[source],
-            device_id=x_device(to), device_id_type=MESH,
-        )
-
-    def pass_on(block):
-        pair_copy(block).wait_recv()
-        for i in range(block_rows // span):
-            to = block * (block_rows // span) + i
-            at = pl.ds(pl.multiple_of(to * span, span), span)
-            x_out[to] = prod[core, at] + pair[at]
+            prod[g, 0, :, at] = total[:block_rows]
+            prod[g, 1, :, at] = total[block_rows:]
+        pair_copy(g).start()
+
+    def x_copy(g, i, to, source, half):
+        return pltpu.make_async_remote_copy(
+            src_ref=x_out.at[g, i], dst_ref=x_in.at[source, half], send_sem=x_send.at[g, i],
+            recv_sem=x_recv.at[source, half], device_id=x_device(to), device_id_type=MESH,
+        )
+
+    def pass_on(g):
+        pair_copy(g).wait_recv()
+        for i in range(size):
+            to, half = source_of(g, i) // 2, source_of(g, i) % 2
+            at = pl.ds(i * vectors, vectors)
+            x_out[g, i] = prod[g, core, at] + pair[g, at]
 
             @pl.when(to != x)
             def _():
-                x_copy(to, x).start()
+                x_copy(g, i, to, x, half).start()
+
+            @pl.when(to == x)
+            def _():
+                x_in[x, half] = x_out[g, i]
 
     @pl.loop(0, GROUPS)
     def _(g):
-        products(arrived(g))
+        products(g)
 
         @pl.when(g > 0)
         def _():
-            pass_on(arrived(g - 1))
-
-    pass_on(arrived(GROUPS - 1))
-
-    total = x_out[x]
-    for step in range(1, X):
-        source = x_peer(step)
-        pltpu.make_async_remote_copy(
-            src_ref=x_out.at[source], dst_ref=x_in.at[source], send_sem=x_send.at[source], recv_sem=x_recv.at[source],
-            device_id=x_device(source), device_id_type=MESH,
-        ).wait_recv()
-        total += x_in[source]
-    for at in range(CORES * Z):
-        z_out[at] = total[2 * at : 2 * at + 2]
+            pass_on(g - 1)
+
+    pass_on(GROUPS - 1)
+
+    @pl.when(has_high)
+    def _():
+        coef_copy(LOW).wait_send()
+
+    @pl.when(has_low)
+    def _():
+        coef_copy(HIGH).wait_send()
+
+    @pl.loop(0, F)
+    def _(step):
+        @pl.when(has_high)
+        def _():
+            halo_copy(LOW, step).wait_send()
+
+        @pl.when(has_low)
+        def _():
+            halo_copy(HIGH, step).wait_send()
+
+    @pl.loop(1, F)
+    def _(step):
+        a2a_copy((f + step) % F, f).wait_send()
+
+    @pl.loop(0, GROUPS)
+    def _(g):
+        pair_copy(g).wait_send()
+
+    for half in range(2):
+        total = x_in[x, half]
+        for step in range(1, X):
+            source = x_peer(step)
+            x_copy(0, 0, source, source, half).wait_recv()
+            total += x_in[source, half]
+        for at in range(vectors // 2):
+            z_out[half * (vectors // 2) + at] = total[2 * at : 2 * at + 2]
 
     def z_copy(to, source):
         return pltpu.make_async_remote_copy(
@@ -343,6 +368,14 @@
         z_copy((local + step) % (CORES * Z), local).start()
 
     z_in[local] = z_out[local]
+
+    for g in range(GROUPS):
+        for i in range(size):
+            to = source_of(g, i) // 2
+
+            @pl.when(to != x)
+            def _():
+                x_copy(g, i, to, x, 0).wait_send()
 
     @pl.loop(1, CORES * Z)
     def _(step):
@@ -355,36 +388,6 @@
             result += z_in[at * CORES + part_at]
         for v in range(2):
             out_ref[v, 0, pl.ds(part_at, 1)] = result[v : v + 1, :sens]
-
-    @pl.when(has_high)
-    def _():
-        coef_copy(LOW).wait_send()
-
-    @pl.when(has_low)
-    def _():
-        coef_copy(HIGH).wait_send()
-
-    @pl.loop(0, GROUPS)
-    def _(g):
-        @pl.when(has_high)
-        def _():
-            halo_copy(LOW, g, (s + 1) // (CORES * Z)).wait_send()
-
-        @pl.when(has_low)
-        def _():
-            halo_copy(HIGH, g, (s - 1) // (CORES * Z)).wait_send()
-
-    @pl.loop(1, F)
-    def _(step):
-        a2a_copy((f + step) % F, f).wait_send()
-
-    @pl.loop(0, GROUPS)
-    def _(block):
-        pair_copy(block).wait_send()
-
-    @pl.loop(1, X)
-    def _(step):
-        x_copy(x_peer(step), x).wait_send()
 
     @pl.loop(1, CORES * Z)
     def _(step):
@@ -398,7 +401,6 @@
     strips = lax.axis_size("seabed")
     X = strips // (Z * CORES)
     all_vectors = vectors * F
-    span = Z * CORES * 2
     sens_pad = -(-sens // 128) * 128
     cells = rows * width
     dims = (X, F, vectors, steps, rows, width, sens, sens_pad)
@@ -423,23 +425,23 @@
             pltpu.VMEM((sens_pad, 2 * cells), BF16),
             pltpu.VMEM((sens_pad, 2 * cells), BF16),
             pltpu.VMEM((2, 2, all_vectors // GROUPS, 2 * cells), BF16),
-            pltpu.VMEM((2, all_vectors, sens_pad), F32),
-            pltpu.VMEM((all_vectors, sens_pad), F32),
-            pltpu.VMEM((X, span, sens_pad), F32),
-            pltpu.VMEM((X, span, sens_pad), F32),
+            pltpu.VMEM((GROUPS, 2, all_vectors // GROUPS, sens_pad), F32),
+            pltpu.VMEM((GROUPS, all_vectors // GROUPS, sens_pad), F32),
+            pltpu.VMEM((GROUPS, F // GROUPS, vectors, sens_pad), F32),
+            pltpu.VMEM((X, 2, vectors, sens_pad), F32),
             pltpu.VMEM((CORES * Z, 2, sens_pad), F32),
             pltpu.VMEM((CORES * Z, 2, sens_pad), F32),
             dma((3,)),
             dma((2,)),
             dma((4,)),
-            dma((2, GROUPS)),
-            dma((2, GROUPS)),
+            dma((2, F)),
+            dma((2, F)),
             dma((F,)),
             dma((F,)),
             dma((GROUPS,)),
             dma((GROUPS,)),
-            dma((X,)),
-            dma((X,)),
+            dma((GROUPS, F // GROUPS)),
+            dma((X, 2)),
             dma((CORES * Z,)),
             dma((CORES * Z,)),
         ],

time: 71.9 us -> 69.5 us (0.967)
  Pallas kernels: 70.1 us -> 68 us
    pallas_call x1, Pallas kernels: 70.1 us -> 68 us  [shards(): pl.pallas_call(functools.partial(kernel, dims), out_shape=jax.ShapeDtypeS...]
where the time goes in v3:
time: 69.5 us; the launch traced here: 69.3 us
  Pallas kernels  68 us (98%)
  local copies, waits for them, and re-layouts  1.3 us (2%)
    pallas_call x1, Pallas kernels, shards(): pl.pallas_call(functools.partial(kernel, dims), out_shape=jax.ShapeDtypeS...  68 us

profile of v3, /device:TPU:1, one launch (start us, length us, event | category | flops | bytes accessed | tf_op | source)
XLA Modules:
  0.0 69.3 jit_solution(7875388535600576760)
XLA Ops:
  0.0 68.0 %shard_map.46 = f32[2,1,2,600]{3,2,1,0:T(2,128)} custom-call(bf16[8,5,32,128]{3,2,1,0:T(8,128)(2,1)} %bitcast.1, f32[5,128]{1,0:T(8,128)} %coef_hbm.1, bf16[2,256,256]{2,1,0:T(8,128)(2,1)} %constant.2.clone.table_hbm, f32[1,2,600,640]{3,2,1,0:T(8,128)} %transfer_ref.1), custom_call_target="tpu_custom_call" | custom-call | tf_op jit(solution)/shard_map/pallas_call | solution.py:411
  68.0 1.3 %copy.6 = f32[2,1,2,600]{3,2,1,0:T(2,128)} copy(f32[2,1,2,600]{3,2,1,0:T(2,128)} %shard_map.46) | data formatting | bytes 19200

commit v4 on v3

--- a/solution.py
+++ b/solution.py
@@ -15,6 +15,7 @@
 Z = 4
 GROUPS = 4
 AHEAD = 16
+WINDOW = 8
 F32 = jnp.float32
 BF16 = jnp.bfloat16
 
@@ -223,6 +224,13 @@
             device_id=(s, k), device_id_type=MESH,
         )
 
+    def a2a_left(step):
+        k = target_of(step)
+
+        @pl.when(k != f)
+        def _():
+            a2a_copy(k, f).wait_send()
+
     @pl.loop(0, F)
     def _(step):
         @pl.when(has_low)
@@ -242,6 +250,10 @@
             at = pl.ds(pl.multiple_of(k * lines + b * vectors, 8), 8)
             for r, value in enumerate(smoothed(at)):
                 outgoing[k, b, r] = value
+
+        @pl.when(step >= WINDOW)
+        def _():
+            a2a_left(step - WINDOW)
 
         @pl.when(k != f)
         def _():
@@ -340,9 +352,9 @@
         def _():
             halo_copy(HIGH, step).wait_send()
 
-    @pl.loop(1, F)
-    def _(step):
-        a2a_copy((f + step) % F, f).wait_send()
+    @pl.loop(F - WINDOW, F)
+    def _(step):
+        a2a_left(step)
 
     @pl.loop(0, GROUPS)
     def _(g):

time: 69.5 us -> 69.2 us (level)
  no operation moved by 1% of the time
where the time goes in v4:
time: 69.2 us; the launch traced here: 69.1 us
  Pallas kernels  67.7 us (98%)
  local copies, waits for them, and re-layouts  1.3 us (2%)
    pallas_call x1, Pallas kernels, shards(): pl.pallas_call(functools.partial(kernel, dims), out_shape=jax.ShapeDtypeS...  67.7 us

profile of v4, /device:TPU:1, one launch (start us, length us, event | category | flops | bytes accessed | tf_op | source)
XLA Modules:
  0.0 69.1 jit_solution(3405775539592618113)
XLA Ops:
  0.0 67.7 %shard_map.46 = f32[2,1,2,600]{3,2,1,0:T(2,128)} custom-call(bf16[8,5,32,128]{3,2,1,0:T(8,128)(2,1)} %bitcast.1, f32[5,128]{1,0:T(8,128)} %coef_hbm.1, bf16[2,256,256]{2,1,0:T(8,128)(2,1)} %constant.2.clone.table_hbm, f32[1,2,600,640]{3,2,1,0:T(8,128)} %transfer_ref.1), custom_call_target="tpu_custom_call" | custom-call | tf_op jit(solution)/shard_map/pallas_call | solution.py:423
  67.8 1.3 %copy.6 = f32[2,1,2,600]{3,2,1,0:T(2,128)} copy(f32[2,1,2,600]{3,2,1,0:T(2,128)} %shard_map.46) | data formatting | bytes 19200
